TPU v7x, 256 devices: a whole 4x4x8 slice. The times are simulated.
256 devices in a mesh: mp: 32 (over z, x), dp: 8 (over y, core).
Axes of the slice: x: 4, y: 4, z: 8, core: 2. Of those that a mesh axis runs over, the one named last changes fastest.
Arguments:
- inputs: bfloat16 [1536, 8192], P('dp', 'mp'), may hold values from -42 to 42
- out_grads: bfloat16 [1536, 16384], P('dp', 'mp'), may hold values from -42 to 42
- weight: bfloat16 [8192, 16384], P('dp', 'mp'), may hold values from -0.25 to 0.25
- enc_in: bfloat16 [8192, 1920], P('mp'), may hold values from -0.0625 to 0.0625
- dec_in: bfloat16 [1920, 8192], P(None, 'mp'), may hold values from -0.125 to 0.125
- enc_out: bfloat16 [16384, 1920], P('mp'), may hold values from -0.046875 to 0.046875
- dec_out: bfloat16 [1920, 16384], P(None, 'mp'), may hold values from -0.125 to 0.125
Outputs:
- post_out: bfloat16 [1536, 16384], P('dp', 'mp')
- grad_in: bfloat16 [1536, 8192], P('dp', 'mp')
All inputs are finite; a program needn't handle non-finite values.
Results may differ from a plain program's by a relative error of at most 0.024.
Values may be sent and summed in bfloat16 or wider, within the bound.
A program may use at most 64 MiB of HBM per device.

v0:
```python
import jax
import jax.numpy as jnp
from jax import lax
from jax.sharding import PartitionSpec as P

D = 8192
FW = 16384
epsilon = 1e-06
step_size = 0.25


def silu_slope(value):
    sig = jax.nn.sigmoid(value)
    return sig * (1.0 + value * (1.0 - sig))


def shards(inputs, out_grads, weight, enc_in, dec_in, enc_out, dec_out):
    factor = step_size / D
    input_wide = inputs.astype(jnp.float32)
    grad_wide = out_grads.astype(jnp.float32)
    input_sq = jnp.sum(input_wide * input_wide, axis=1)
    grad_sq = jnp.sum(grad_wide * grad_wide, axis=1)
    input_proj = jnp.dot(inputs, enc_in, preferred_element_type=jnp.float32)
    grad_proj = jnp.dot(out_grads, enc_out, preferred_element_type=jnp.float32)
    input_total, grad_total = lax.psum((input_sq, grad_sq), "mp")
    input_proj, grad_proj = (
        lax.psum(input_proj.astype(jnp.bfloat16), "mp").astype(jnp.float32),
        lax.psum(grad_proj.astype(jnp.bfloat16), "mp").astype(jnp.float32),
    )
    input_scale = lax.rsqrt(input_total / D + epsilon)[:, None]
    grad_scale = lax.rsqrt(grad_total / FW + epsilon)[:, None]
    input_hidden = jax.nn.relu(input_proj * input_scale).astype(jnp.bfloat16)
    grad_hidden = jax.nn.relu(grad_proj * grad_scale).astype(jnp.bfloat16)
    edited_in = (
        input_wide + jnp.dot(input_hidden, dec_in, preferred_element_type=jnp.float32)
    ).astype(jnp.bfloat16)
    edited_grad = (
        grad_wide + jnp.dot(grad_hidden, dec_out, preferred_element_type=jnp.float32)
    ).astype(jnp.bfloat16)
    whole_in = lax.all_gather(inputs, "mp", axis=1, tiled=True)
    edits_all = lax.all_gather(edited_in, "dp", axis=0, tiled=True)
    grads_all = lax.all_gather(edited_grad, "dp", axis=0, tiled=True)
    kernel = lax.psum(
        jnp.dot(inputs, edits_all.T, preferred_element_type=jnp.float32).astype(jnp.bfloat16), "mp"
    ).astype(jnp.float32)
    kernel = (kernel * factor).astype(jnp.bfloat16)
    base_out = jnp.dot(
        whole_in,
        lax.all_gather(weight, "dp", axis=0, tiled=True),
        preferred_element_type=jnp.float32,
    )
    post_full = base_out - jnp.dot(kernel, grads_all, preferred_element_type=jnp.float32)
    cotangent = (grad_wide * silu_slope(post_full)).astype(jnp.bfloat16)
    back_kernel = lax.psum(
        jnp.dot(cotangent, grads_all.T, preferred_element_type=jnp.float32).astype(jnp.bfloat16),
        "mp",
    ).astype(jnp.float32)
    back_kernel = (back_kernel * factor).astype(jnp.bfloat16)
    partial_value = jnp.dot(
        cotangent,
        lax.all_gather(weight, "dp", axis=0, tiled=True).T,
        preferred_element_type=jnp.float32,
    )
    back_sum = lax.psum_scatter(
        partial_value.astype(jnp.bfloat16), "mp", scatter_dimension=1, tiled=True
    ).astype(jnp.float32)
    grad_in = (
        back_sum - jnp.dot(back_kernel, edits_all, preferred_element_type=jnp.float32)
    ).astype(jnp.bfloat16)
    return (post_full.astype(jnp.bfloat16), grad_in)


def solution(mesh):
    in_specs = (
        P("dp", "mp"),
        P("dp", "mp"),
        P("dp", "mp"),
        P("mp", None),
        P(None, "mp"),
        P("mp", None),
        P(None, "mp"),
    )
    out_specs = (P("dp", "mp"), P("dp", "mp"))
    return jax.shard_map(shards, mesh=mesh, in_specs=in_specs, out_specs=out_specs, check_vma=False)
```

profile of v0, /device:TPU:8, one launch (start us, length us, event | category | flops | bytes accessed | tf_op | source)
XLA Modules:
  0.0 874.0 jit_solution(16068317335428372301)
XLA Ops:
  7.2 0.0 all-reduce.6.cloned.1.call-start
  7.2 2.7 convolution_convert_fusion.4
  9.9 0.0 all-reduce.6.cloned.1.call-update
  9.9 0.0 all-reduce.10.cloned.1.call-start
  10.0 0.1 fusion.12
  10.1 0.1 fusion.10
  10.2 77.8 %all-reduce = (f32[192]{0:T(256)S(1)}, f32[192]{0:T(256)S(1)}) all-reduce(f32[192]{0:T(256)S(1)} %fusion.10, f32[192]{0:T(256)S(1)} %fusion.12), channel_id=1, replica_groups=mesh['mp'=32,'dp'=8] {'mp'}, use_global_device_ids=true, to_apply=%region_6.7 | all-reduce | flops 384 | bytes 3072 | tf_op jit(solution)/shard_map/psum | solution.py:25
  88.0 1.5 convolution_convert_fusion.3
  89.5 73.4 %all-reduce.6.cloned.1.call-done = bf16[192,1920]{1,0:T(8,128)(2,1)} async-done(((bf16[192,1920]{1,0:T(8,128)(2,1)}), bf16[192,1920]{1,0:T(8,128)(2,1)}) %all-reduce.6.cloned.1.call-update) | async-done | bytes 737296 | tf_op jit(solution)/shard_map/psum | solution.py:27
  162.9 1.9 fusion.2
  164.8 13.5 %all_gather.15 = bf16[1536,256]{1,0:T(8,128)(2,1)S(1)} all-gather(bf16[192,256]{1,0:T(8,128)(2,1)S(1)} %fusion.2), channel_id=1, replica_groups=mesh['mp'=32,'dp'=8] {'dp'}, dimensions={0}, use_global_device_ids=true | all-gather | bytes 884736 | tf_op jit(solution)/shard_map/all_gather | solution.py:41
  178.3 1.3 fusion
  179.6 0.0 all-reduce.10.cloned.1.call-update
  179.6 0.0 all-gather.4.cloned.1.call-start
  179.7 0.7 all-gather.4.cloned.1.call-update
  180.4 0.0 all-gather.6.cloned.1.call-start
  180.4 0.5 all-gather.6.cloned.1.call-update
  180.9 0.0 all-gather.8.cloned.1.call-start
  181.0 147.2 %all-reduce.10.cloned.1.call-done = (bf16[192,1920]{1,0:T(8,128)(2,1)}, bf16[192,1536]{0,1:T(8,128)(2,1)}) async-done(((bf16[192,1920]{1,0:T(8,128)(2,1)}, bf16[192,1536]{0,1:T(8,128)(2,1)}), (bf16[192,1920]{1,0:T(8,128)(2,1)}, bf16[192,1536]{0,1:T(8,128)(2,1)})) %all-reduce.10.cloned.1.call-update) | async-done | bytes 1327120 | tf_op jit(solution)/shard_map/psum | solution.py:28
  328.2 3.1 fusion.1
  331.3 0.0 all-reduce.8.cloned.1.call-start
  331.4 75.0 %all-gather.4.cloned.1.call-done = bf16[192,8192]{1,0:T(8,128)(2,1)} async-done(((bf16[192,256]{1,0:T(8,128)(2,1)}), bf16[192,8192]{1,0:T(8,128)(2,1)}) %all-gather.4.cloned.1.call-update) | async-done | bytes 3145744 | tf_op jit(solution)/shard_map/all_gather | solution.py:40
  406.4 53.9 %all-gather.6.cloned.1.call-done = bf16[8192,512]{1,0:T(8,128)(2,1)} async-done(((bf16[1024,512]{1,0:T(8,128)(2,1)}), bf16[8192,512]{1,0:T(8,128)(2,1)}) %all-gather.6.cloned.1.call-update) | async-done | bytes 8388624 | tf_op jit(solution)/shard_map/all_gather | solution.py:49
  460.3 6.9 fusion.20
  467.2 22.0 %all-gather.8.cloned.1.call-done = bf16[1536,512]{1,0:T(8,128)(2,1)} async-done(((bf16[192,512]{1,0:T(8,128)(2,1)}), bf16[1536,512]{1,0:T(8,128)(2,1)}) %all-gather.8.cloned.1.call-update) | async-done | bytes 1572880 | tf_op jit(solution)/shard_map/all_gather | solution.py:42
  489.2 2.9 fusion.19
  492.1 2.6 convolution_convert_fusion.2
  494.8 0.0 reduce-scatter.2.cloned.1.call-start
  494.9 8.1 convolution_convert_fusion
  503.0 142.1 %all-reduce.8.cloned.1.call-done = bf16[192,1536]{0,1:T(8,128)(2,1)} async-done(((bf16[192,1536]{0,1:T(8,128)(2,1)}), bf16[192,1536]{0,1:T(8,128)(2,1)}) %all-reduce.8.cloned.1.call-update) | async-done | bytes 589840 | tf_op jit(solution)/shard_map/psum | solution.py:54
  645.1 219.9 %reduce-scatter.2.cloned.1.call-done = bf16[192,256]{1,0:T(8,128)(2,1)} async-done(((bf16[192,8192]{1,0:T(8,128)(2,1)}), bf16[192,256]{1,0:T(8,128)(2,1)}) %reduce-scatter.2.cloned.1.call-update) | async-done | bytes 98320 | tf_op jit(solution)/shard_map/reduce_scatter | solution.py:64
  865.0 2.2 fusion.3
  (19 shorter events, 0.1 us)
Async XLA Ops:
  7.2 80.9 %copy-start = (bf16[512,1920]{1,0:T(8,128)(2,1)S(1)}, bf16[512,1920]{1,0:T(8,128)(2,1)}, u32[]{:S(2)}) copy-start(bf16[512,1920]{1,0:T(8,128)(2,1)} %param.12) | copy-start | bytes 5898244
  7.2 2.8 copy-start.1
  7.2 2.9 copy-start.4
  7.2 155.7 %all-reduce.6.cloned.1.call-start = ((), (), s32[]{:S(2)}) async-start(), calls=%async_computation.3 | async-start | bytes 1474560 | tf_op jit(solution)/shard_map/psum | solution.py:27
  9.9 318.3 %all-reduce.10.cloned.1.call-start = ((), (), s32[]{:S(2)}) async-start(), calls=%async_computation.7 | async-start | bytes 3047424 | tf_op jit(solution)/shard_map/psum | solution.py:28
  179.6 226.8 %all-gather.4.cloned.1.call-start = ((), (), s32[]{:S(2)}) async-start(), calls=%async_computation.1 | async-start | bytes 3244032 | tf_op jit(solution)/shard_map/all_gather | solution.py:40
  180.4 280.0 %all-gather.6.cloned.1.call-start = ((), (), s32[]{:S(2)}) async-start(), calls=%async_computation.2 | async-start | bytes 9437184 | tf_op jit(solution)/shard_map/all_gather | solution.py:49
  180.9 308.3 %all-gather.8.cloned.1.call-start = ((), (), s32[]{:S(2)}) async-start(), calls=%async_computation.4 | async-start | bytes 1769472 | tf_op jit(solution)/shard_map/all_gather | solution.py:42
  331.3 157.9 %copy-start.3 = (bf16[192,1536]{0,1:T(8,128)(2,1)S(1)}, bf16[192,1536]{0,1:T(8,128)(2,1)}, u32[]{:S(2)}) copy-start(bf16[192,1536]{0,1:T(8,128)(2,1)} %get-tuple-element.5) | copy-start | bytes 1769476
  331.3 313.8 %all-reduce.8.cloned.1.call-start = ((), (), s32[]{:S(2)}) async-start(), calls=%async_computation.6 | async-start | bytes 1572864 | tf_op jit(solution)/shard_map/psum | solution.py:54
  489.2 2.9 copy-start.2
  489.2 2.9 copy-start.5
  492.1 2.7 copy-start.6
  494.8 370.2 %reduce-scatter.2.cloned.1.call-start = ((), (), s32[]{:S(2)}) async-start(), calls=%async_computation.5 | async-start | bytes 3244032 | tf_op jit(solution)/shard_map/reduce_scatter | solution.py:64
Sparse Core Ops, SparseCore 0:
  11.4 151.4 all-reduce.5
  179.7 148.4 all-reduce.9
  331.0 75.3 all-gather.3
  408.3 51.9 all-gather.5
  462.7 26.4 all-gather.7
  494.9 150.1 all-reduce.7
  649.5 215.4 reduce-scatter.1
where the time goes:
time: 874 us
  waiting for transfers between devices  735 us (84%)
  blocking collectives  91.3 us (10%)
  matrix products  33.1 us (4%)
  between operations  14.2 us (2%)
    reduce_scatter x1, waiting for transfers between devices, shards(): lax.psum_scatter(partial_value.astype(jnp.bfloat16), 'mp', scatter_dimens...  220 us
    psum x1, waiting for transfers between devices, shards(): lax.psum(grad_proj.astype(jnp.bfloat16), 'mp').astype(jnp.float32)  147 us
    psum x1, waiting for transfers between devices, shards(): lax.psum(jnp.dot(cotangent, grads_all.T, preferred_element_type=jnp.float...  142 us
    psum x1, blocking collectives, shards(): input_total, grad_total = lax.psum((input_sq, grad_sq), 'mp')  77.8 us
    all_gather x1, waiting for transfers between devices, shards(): whole_in = lax.all_gather(inputs, 'mp', axis=1, tiled=True)  75 us
    psum x1, waiting for transfers between devices, shards(): lax.psum(input_proj.astype(jnp.bfloat16), 'mp').astype(jnp.float32)  73.4 us
    all_gather x1, waiting for transfers between devices, shards(): lax.all_gather(weight, 'dp', axis=0, tiled=True)  53.9 us
    all_gather x1, waiting for transfers between devices, shards(): grads_all = lax.all_gather(edited_grad, 'dp', axis=0, tiled=True)  22 us
  transfers between devices with their start and end apart: 7, of which 7 were waited for; matrix products, arithmetic and copies ran while one was open for 2% of the time, Pallas kernels for 0%

commit v1 on v0

--- a/solution.py
+++ b/solution.py
@@ -37,7 +37,9 @@
     edited_grad = (
         grad_wide + jnp.dot(grad_hidden, dec_out, preferred_element_type=jnp.float32)
     ).astype(jnp.bfloat16)
-    whole_in = lax.all_gather(inputs, "mp", axis=1, tiled=True)
+    whole_in = jnp.concatenate(
+        lax.all_to_all(jnp.stack([inputs] * lax.axis_size("mp")), "mp", 0, 0), axis=1
+    )
     edits_all = lax.all_gather(edited_in, "dp", axis=0, tiled=True)
     grads_all = lax.all_gather(edited_grad, "dp", axis=0, tiled=True)
     kernel = lax.psum(

time: 874 us -> 767 us (0.88)
  waiting for transfers between devices: 735 us -> 616 us
    all_gather x1 -> x0, waiting for transfers between devices: 75 us -> none  [shards(): whole_in = lax.all_gather(inputs, 'mp', axis=1, tiled=True)]
    all_gather x1, waiting for transfers between devices: 53.9 us -> 0.01 us  [shards(): lax.all_gather(weight, 'dp', axis=0, tiled=True)]
    psum x1, waiting for transfers between devices: 147 us -> 170 us  [shards(): lax.psum(grad_proj.astype(jnp.bfloat16), 'mp').astype(jnp.float32)]
    all_gather x1, waiting for transfers between devices: 22 us -> 11.3 us  [shards(): grads_all = lax.all_gather(edited_grad, 'dp', axis=0, tiled=True)]
  transfers between devices with their start and end apart: 7 -> 7, of which waited for: 7 -> 5; matrix products, arithmetic and copies ran while one was open for 2% -> 3% of each run, Pallas kernels for 0% -> 0%
where the time goes in v1:
time: 767 us; the launch traced here: 766 us
  waiting for transfers between devices  616 us (80%)
  blocking collectives  91.3 us (12%)
  matrix products  31.6 us (4%)
  between operations  15.3 us (2%)
    reduce_scatter x1, waiting for transfers between devices, shards(): lax.psum_scatter(partial_value.astype(jnp.bfloat16), 'mp', scatter_dimens...  220 us
    psum x1, waiting for transfers between devices, shards(): lax.psum(grad_proj.astype(jnp.bfloat16), 'mp').astype(jnp.float32)  170 us
    psum x1, waiting for transfers between devices, shards(): lax.psum(jnp.dot(cotangent, grads_all.T, preferred_element_type=jnp.float...  141 us
    psum x1, blocking collectives, shards(): input_total, grad_total = lax.psum((input_sq, grad_sq), 'mp')  77.8 us
    psum x1, waiting for transfers between devices, shards(): lax.psum(input_proj.astype(jnp.bfloat16), 'mp').astype(jnp.float32)  73.4 us
  transfers between devices with their start and end apart: 7, of which 5 were waited for; matrix products, arithmetic and copies ran while one was open for 3% of the time, Pallas kernels for 0%

profile of v1, /device:TPU:8, one launch (start us, length us, event | category | flops | bytes accessed | tf_op | source)
XLA Modules:
  0.0 766.2 jit_solution(4736075670951551556)
XLA Ops:
  8.0 0.0 all-reduce.6.cloned.1.call-start
  8.1 2.7 convolution_convert_fusion.3
  10.8 0.0 all-reduce.10.cloned.1.call-start
  10.8 0.1 fusion.12
  10.9 0.1 fusion.10
  11.1 77.8 %all-reduce = (f32[192]{0:T(256)S(1)}, f32[192]{0:T(256)S(1)}) all-reduce(f32[192]{0:T(256)S(1)} %fusion.10, f32[192]{0:T(256)S(1)} %fusion.12), channel_id=1, replica_groups=mesh['mp'=32,'dp'=8] {'mp'}, use_global_device_ids=true, to_apply=%region_6.7 | all-reduce | flops 384 | bytes 3072 | tf_op jit(solution)/shard_map/psum | solution.py:25
  88.9 1.5 convolution_convert_fusion.1
  90.3 73.4 %all-reduce.6.cloned.1.call-done = bf16[192,1920]{1,0:T(8,128)(2,1)} async-done(((bf16[192,1920]{1,0:T(8,128)(2,1)}), bf16[192,1920]{1,0:T(8,128)(2,1)}) %all-reduce.6.cloned.1.call-update) | async-done | bytes 737296 | tf_op jit(solution)/shard_map/psum | solution.py:27
  163.8 1.8 fusion.2
  165.6 13.5 %all_gather.11 = bf16[1536,256]{1,0:T(8,128)(2,1)S(1)} all-gather(bf16[192,256]{1,0:T(8,128)(2,1)S(1)} %fusion.2), channel_id=1, replica_groups=mesh['mp'=32,'dp'=8] {'dp'}, dimensions={0}, use_global_device_ids=true | all-gather | bytes 884736 | tf_op jit(solution)/shard_map/all_gather | solution.py:43
  179.2 1.2 fusion
  180.4 0.0 all-reduce.10.cloned.1.call-update
  180.4 0.0 all-gather.3.cloned.1.call-start
  180.5 0.5 all-gather.3.cloned.1.call-update
  181.0 2.1 stack.2
  183.1 5.5 all-to-all-start
  188.5 0.0 all-gather.5.cloned.1.call-start
  188.6 169.7 %all-reduce.10.cloned.1.call-done = (bf16[192,1920]{1,0:T(8,128)(2,1)}, bf16[192,1536]{1,0:T(8,128)(2,1)}) async-done(((bf16[192,1920]{1,0:T(8,128)(2,1)}, bf16[192,1536]{1,0:T(8,128)(2,1)}), (bf16[192,1920]{1,0:T(8,128)(2,1)}, bf16[192,1536]{1,0:T(8,128)(2,1)})) %all-reduce.10.cloned.1.call-update) | async-done | bytes 1327120 | tf_op jit(solution)/shard_map/psum | solution.py:28
  358.3 3.1 fusion.1
  361.4 0.0 all-gather.5.cloned.1.call-update
  361.4 0.0 all-reduce.8.cloned.1.call-start
  361.5 4.0 copy.10
  365.4 6.9 fusion.20
  372.4 11.3 %all-gather.5.cloned.1.call-done = bf16[1536,512]{1,0:T(8,128)(2,1)} async-done(((bf16[192,512]{1,0:T(8,128)(2,1)}), bf16[1536,512]{1,0:T(8,128)(2,1)}) %all-gather.5.cloned.1.call-update) | async-done | bytes 1572880 | tf_op jit(solution)/shard_map/all_gather | solution.py:44
  383.7 2.9 fusion.19
  386.6 1.5 convolution_convert_fusion.4
  388.1 0.0 all-reduce.8.cloned.1.call-update
  388.1 0.0 reduce-scatter.2.cloned.1.call-start
  388.2 8.0 %convolution_convert_fusion = bf16[192,8192]{1,0:T(8,128)(2,1)} fusion(bf16[8192,512]{1,0:T(8,128)(2,1)} %all-gather.3.cloned.1.call-done, bf16[192,512]{1,0:T(8,128)(2,1)S(1)} %copy-done.3, f32[192,512]{1,0:T(8,128)S(1)} %get-tuple-element.7), kind=kOutput, calls=%fused_computation | convolution fusion | flops 1613168640 | bytes 12124160 | tf_op jit(solution)/shard_map/dot_general | solution.py:61
  396.2 141.3 %all-reduce.8.cloned.1.call-done = bf16[192,1536]{1,0:T(8,128)(2,1)} async-done(((bf16[192,1536]{1,0:T(8,128)(2,1)}), bf16[192,1536]{1,0:T(8,128)(2,1)}) %all-reduce.8.cloned.1.call-update) | async-done | bytes 589840 | tf_op jit(solution)/shard_map/psum | solution.py:56
  537.5 219.6 %reduce-scatter.2.cloned.1.call-done = bf16[192,256]{1,0:T(8,128)(2,1)} async-done(((bf16[192,8192]{1,0:T(8,128)(2,1)}), bf16[192,256]{1,0:T(8,128)(2,1)}) %reduce-scatter.2.cloned.1.call-update) | async-done | bytes 98320 | tf_op jit(solution)/shard_map/reduce_scatter | solution.py:66
  757.1 2.0 fusion.3
  (14 shorter events, 0.1 us)
Async XLA Ops:
  8.0 80.9 %copy-start = (bf16[512,1920]{1,0:T(8,128)(2,1)S(1)}, bf16[512,1920]{1,0:T(8,128)(2,1)}, u32[]{:S(2)}) copy-start(bf16[512,1920]{1,0:T(8,128)(2,1)} %param.12) | copy-start | bytes 5898244
  8.0 2.8 copy-start.1
  8.0 2.9 copy-start.3
  8.0 155.7 %all-reduce.6.cloned.1.call-start = ((), (), s32[]{:S(2)}) async-start(), calls=%async_computation.3 | async-start | bytes 1474560 | tf_op jit(solution)/shard_map/psum | solution.py:27
  10.8 347.5 %all-reduce.10.cloned.1.call-start = ((), (), s32[]{:S(2)}) async-start(), calls=%async_computation.7 | async-start | bytes 2654208 | tf_op jit(solution)/shard_map/psum | solution.py:28
  180.4 185.0 %all-gather.3.cloned.1.call-start = ((), (), s32[]{:S(2)}) async-start(), calls=%async_computation.2 | async-start | bytes 9437184 | tf_op jit(solution)/shard_map/all_gather | solution.py:51
  183.1 178.4 %all-to-all-start = ((bf16[32,192,256]{2,1,0:T(8,128)(2,1)}), bf16[32,192,256]{2,1,0:T(8,128)(2,1)}, u32[]{:S(2)}, u32[]{:S(2)}) async-start(bf16[32,192,256]{2,1,0:T(8,128)(2,1)} %stack.2), calls=%async_computation | async-start | bytes 6291456 | tf_op jit(solution)/shard_map/all_to_all | solution.py:41
  188.5 195.1 %all-gather.5.cloned.1.call-start = ((), (), s32[]{:S(2)}) async-start(), calls=%async_computation.4 | async-start | bytes 1769472 | tf_op jit(solution)/shard_map/all_gather | solution.py:44
  361.4 176.1 %all-reduce.8.cloned.1.call-start = ((), (), s32[]{:S(2)}) async-start(), calls=%async_computation.6 | async-start | bytes 1179648 | tf_op jit(solution)/shard_map/psum | solution.py:56
  383.7 2.9 copy-start.2
  388.1 368.9 %reduce-scatter.2.cloned.1.call-start = ((), (), s32[]{:S(2)}) async-start(), calls=%async_computation.5 | async-start | bytes 3244032 | tf_op jit(solution)/shard_map/reduce_scatter | solution.py:66
Sparse Core Ops, SparseCore 0:
  12.3 151.4 all-reduce.5
  180.5 177.7 all-reduce.9
  388.3 149.1 all-reduce.7
  541.2 215.8 reduce-scatter.1
Sparse Core Ops, SparseCore 1:
  182.7 47.8 all-gather.2
  361.5 22.1 all-gather.4
